TPU v7x, 32 devices: a whole 2x2x4 slice. The times are simulated.
32 devices in a mesh: seq: 4 (over y, x), tensor: 8 (over z, core).
Axes of the slice: x: 2, y: 2, z: 4, core: 2. Of those that a mesh axis runs over, the one named last changes fastest.
Arguments:
- queries: bfloat16 [4096, 4096], P(('seq', 'tensor')), may hold values from -6 to 6
- key_rows: bfloat16 [4096, 4096], P(('seq', 'tensor')), may hold values from -6 to 6
- values: bfloat16 [4096, 4096], P(('seq', 'tensor')), may hold values from -6 to 6
- input_gate: bfloat16 [4096, 4], P(('seq', 'tensor')), may hold values from -3 to 1
- forget_gate: bfloat16 [4096, 4], P(('seq', 'tensor')), may hold values from 0 to 16
- segment_ids: int32 [4096], P('seq'), may hold values from 0 to 3, never falling along the last dimension, each value on 1 to 2048 neighbouring positions
- output_gate: bfloat16 [4096, 4096], P(('seq', 'tensor')), may hold values from -6 to 6
- norm_gain: float32 [4096], replicated, may hold values from 0.5 to 1.5
Outputs:
- gated_out: bfloat16 [4096, 4096], P(('seq', 'tensor'))
Inputs may be any that keep to these rules, and one draw needn't show every extreme that they name: `segment_ids`: non-decreasing along the tokens; each of the 4 prompts holds 1 to 2048 consecutive tokens, one exactly 2048.
All inputs are finite; a program needn't handle non-finite values.
Results may differ from a plain program's by a relative error of at most 0.005.
Values may be sent and summed in bfloat16 or wider, within the bound.
A program may use at most 64 MiB of HBM per device.

v0:
```python
import math

import jax
import jax.numpy as jnp
from jax import lax
from jax.sharding import PartitionSpec as P

BLOCK = 256


precise = lax.Precision.HIGHEST


def shifted(value, axis, steps):
    count = lax.axis_size(axis)
    initial, last = (max(0, -steps), min(count, count - steps))
    return lax.ppermute(value, axis, [(source, source + steps) for source in range(initial, last)])


def combine_states(earlier, later):
    e_decay, e_state, e_norm, e_first, e_last = earlier
    l_decay, l_state, l_norm, l_first, l_last = later
    linked = jnp.where((e_last == l_first) | (e_last <= 0.0) | (l_first <= 0.0), 1.0, 0.0)
    factor = jnp.where(l_first <= 0.0, 1.0, l_decay * linked)
    decay_part = jnp.where(e_first <= 0.0, l_decay, e_decay * factor)
    state_part = factor * e_state + l_state
    norm_part = factor * e_norm + l_norm
    first_seg = jnp.where(e_first <= 0.0, l_first, e_first)
    last_seg = jnp.where(l_last <= 0.0, e_last, l_last)
    return (decay_part, state_part, norm_part, first_seg, last_seg)


def on_device(
    queries, key_rows, values, input_gate, forget_gate, segment_ids, output_gate, norm_gain
):
    tensor_size = lax.axis_size("tensor")
    row_count, inner = queries.shape
    head_count = input_gate.shape[1]
    head_dim = inner // head_count
    group_size = tensor_size // head_count
    column_count = head_dim // group_size

    def spread_heads(array, width):
        shaped = array.reshape(row_count, head_count, 1, width)
        return jnp.broadcast_to(shaped, (row_count, head_count, group_size, width)).reshape(
            row_count, tensor_size, width
        )

    query_send = spread_heads(queries, head_dim)
    key_send = spread_heads(key_rows, head_dim)
    value_send = values.reshape(row_count, tensor_size, column_count)
    gate_send = spread_heads(jnp.stack([input_gate, forget_gate], axis=2), 2)
    query_all, key_all, value_all, gate_all = (
        lax.all_to_all(query_send, "tensor", split_axis=1, concat_axis=0, tiled=True),
        lax.all_to_all(key_send, "tensor", split_axis=1, concat_axis=0, tiled=True),
        lax.all_to_all(value_send, "tensor", split_axis=1, concat_axis=0, tiled=True),
        lax.all_to_all(gate_send, "tensor", split_axis=1, concat_axis=0, tiled=True),
    )
    token_count = query_all.shape[0]
    query_all = query_all.reshape(token_count, head_dim)
    key_all = key_all.reshape(token_count, head_dim)
    value_all = value_all.reshape(token_count, column_count)
    gate_f = gate_all.reshape(token_count, 2).astype(jnp.float32)
    gate_in = gate_f[:, 0]
    log_forget = jax.nn.log_sigmoid(gate_f[:, 1])
    block_count = token_count // BLOCK
    key_scale = 1.0 / math.sqrt(head_dim)
    first_seg = segment_ids[0]
    row_ids = jnp.arange(BLOCK, dtype=jnp.int32)
    causal = row_ids[:, None] >= row_ids[None, :]

    def span_step(carry, block_in):
        cell_state, norm_vec, prev_seg, total_log = carry
        query_b, key_b, value_b, gate_b, forget_b, seg_b = block_in
        cumulative = jnp.cumsum(forget_b)
        allowed = causal & (seg_b[:, None] == seg_b[None, :])
        exponent = cumulative[:, None] - cumulative[None, :] + gate_b[None, :]
        weights = jnp.where(allowed, jnp.exp(jnp.where(allowed, exponent, 0.0)), 0.0)
        scores = (
            jnp.einsum("id,jd->ij", query_b, key_b, preferred_element_type=jnp.float32) * key_scale
        )
        weighted = weights * scores
        query_float = query_b.astype(jnp.float32)
        key_f = key_b.astype(jnp.float32) * key_scale
        value_f = value_b.astype(jnp.float32)
        numerator = jnp.dot(weighted, value_f, precision=precise)
        carried = jnp.exp(cumulative) * (seg_b == prev_seg).astype(jnp.float32)
        numerator = numerator + carried[:, None] * jnp.dot(
            query_float, cell_state, precision=precise
        )
        q_norm = jnp.sum(weighted, axis=1) + carried * jnp.dot(
            query_float, norm_vec, precision=precise
        )
        entry_factor = jnp.exp(total_log + cumulative) * (seg_b == first_seg).astype(jnp.float32)
        last_seg = seg_b[BLOCK - 1]
        tail_weight = jnp.exp(cumulative[BLOCK - 1] - cumulative + gate_b) * (
            seg_b == last_seg
        ).astype(jnp.float32)
        keep_factor = jnp.exp(cumulative[BLOCK - 1]) * (last_seg == prev_seg).astype(jnp.float32)
        scaled_keys = key_f * tail_weight[:, None]
        cell_state = keep_factor * cell_state + jnp.dot(scaled_keys.T, value_f, precision=precise)
        norm_vec = keep_factor * norm_vec + jnp.sum(scaled_keys, axis=0)
        return (
            (cell_state, norm_vec, last_seg, total_log + cumulative[BLOCK - 1]),
            (numerator, q_norm, entry_factor),
        )

    initial = (
        jnp.zeros((head_dim, column_count), jnp.float32),
        jnp.zeros((head_dim,), jnp.float32),
        first_seg,
        jnp.zeros((), jnp.float32),
    )
    blocks_in = (
        query_all.reshape(block_count, BLOCK, head_dim),
        key_all.reshape(block_count, BLOCK, head_dim),
        value_all.reshape(block_count, BLOCK, column_count),
        gate_in.reshape(block_count, BLOCK),
        log_forget.reshape(block_count, BLOCK),
        segment_ids.reshape(block_count, BLOCK),
    )
    final_carry, outputs = lax.scan(span_step, initial, blocks_in)
    cell_state, norm_vec, last_seg, total_log = final_carry
    numerator = outputs[0].reshape(token_count, column_count)
    q_norm = outputs[1].reshape(token_count)
    entry_factor = outputs[2].reshape(token_count)
    summary = (
        jnp.reshape(jnp.exp(total_log) * (last_seg == first_seg).astype(jnp.float32), (1,)),
        cell_state,
        norm_vec,
        jnp.reshape((first_seg + 1).astype(jnp.float32), (1,)),
        jnp.reshape((last_seg + 1).astype(jnp.float32), (1,)),
    )
    empty = jax.tree.map(jnp.zeros_like, summary)

    def relay_step(index, incoming):
        return shifted(combine_states(incoming, summary), "seq", 1)

    incoming = lax.fori_loop(0, lax.axis_size("seq") - 1, relay_step, empty)
    in_decay, in_state, in_norm, in_first, in_last = incoming
    linked = (in_last == summary[3]).astype(jnp.float32)
    scale_rows = entry_factor * linked
    query_full = query_all.astype(jnp.float32)
    numerator = numerator + scale_rows[:, None] * jnp.dot(query_full, in_state, precision=precise)
    q_norm = q_norm + scale_rows * jnp.dot(query_full, in_norm, precision=precise)
    hidden = (numerator / jnp.maximum(jnp.abs(q_norm), 1.0)[:, None]).astype(jnp.bfloat16)
    returned = lax.all_to_all(
        hidden.reshape(token_count, 1, column_count),
        "tensor",
        split_axis=0,
        concat_axis=1,
        tiled=True,
    )
    hidden_f = returned.astype(jnp.float32).reshape(row_count, head_count, head_dim)
    mean_val = jnp.mean(hidden_f, axis=2, keepdims=True)
    centered = hidden_f - mean_val
    variance = jnp.mean(centered * centered, axis=2, keepdims=True)
    normed = (centered * lax.rsqrt(variance + 1e-05)).reshape(row_count, inner)
    return (normed * norm_gain * jax.nn.silu(output_gate.astype(jnp.float32))).astype(jnp.bfloat16)


def solution(mesh):
    in_specs = (
        P(("seq", "tensor"), None),
        P(("seq", "tensor"), None),
        P(("seq", "tensor"), None),
        P(("seq", "tensor"), None),
        P(("seq", "tensor"), None),
        P("seq"),
        P(("seq", "tensor"), None),
        P(),
    )
    out_specs = P(("seq", "tensor"), None)
    return jax.shard_map(
        on_device, mesh=mesh, in_specs=in_specs, out_specs=out_specs, check_vma=False
    )
```

profile of v0, /device:TPU:17, one launch (start us, length us, event | category | flops | bytes accessed | tf_op | source)
XLA Modules:
  0.0 459.6 jit_solution(3974509525305194166)
XLA Ops:
  1.3 5.5 %all-to-all-start = ((bf16[128,8,2]{0,2,1:T(2,128)(2,1)}), bf16[128,8,2]{0,2,1:T(2,128)(2,1)S(1)}, u32[]{:S(2)}, u32[]{:S(2)}) async-start(bf16[128,8,2]{0,2,1:T(2,128)(2,1)} %bitcast.4), calls=%async_computation | async-start | bytes 8192 | tf_op jit(solution)/shard_map/all_to_all | solution.py:57
  6.8 2.4 copy.43
  9.5 6.3 %all-to-all-start.2 = ((bf16[128,8,512]{2,0,1:T(8,128)(2,1)}), bf16[128,8,512]{2,0,1:T(8,128)(2,1)S(1)}, u32[]{:S(2)}, u32[]{:S(2)}) async-start(bf16[128,8,512]{2,0,1:T(8,128)(2,1)} %bitcast.127), calls=%async_computation.2 | async-start | bytes 2097152 | tf_op jit(solution)/shard_map/all_to_all | solution.py:56
  16.0 22.7 %all-to-all-done.2 = bf16[128,8,512]{2,0,1:T(8,128)(2,1)S(1)} async-done(((bf16[128,8,512]{2,0,1:T(8,128)(2,1)}), bf16[128,8,512]{2,0,1:T(8,128)(2,1)S(1)}, u32[]{:S(2)}, u32[]{:S(2)}) %all-to-all-start.2) | async-done | bytes 1048608 | tf_op jit(solution)/shard_map/all_to_all | solution.py:56
  38.7 1.6 broadcast_in_dim.64
  40.3 7.3 %all-to-all-start.3 = ((bf16[128,8,1024]{2,0,1:T(8,128)(2,1)}), bf16[128,8,1024]{2,0,1:T(8,128)(2,1)S(1)}, u32[]{:S(2)}, u32[]{:S(2)}) async-start(bf16[128,8,1024]{2,0,1:T(8,128)(2,1)} %bitcast.199), calls=%async_computation.3 | async-start | bytes 4194304 | tf_op jit(solution)/shard_map/all_to_all | solution.py:54
  47.6 2.3 copy.44
  49.9 43.0 %all-to-all-done.3 = bf16[128,8,1024]{2,0,1:T(8,128)(2,1)S(1)} async-done(((bf16[128,8,1024]{2,0,1:T(8,128)(2,1)}), bf16[128,8,1024]{2,0,1:T(8,128)(2,1)S(1)}, u32[]{:S(2)}, u32[]{:S(2)}) %all-to-all-start.3) | async-done | bytes 2097184 | tf_op jit(solution)/shard_map/all_to_all | solution.py:54
  92.9 3.6 broadcast_in_dim.62
  96.5 8.2 %all-to-all-start.1 = ((bf16[128,8,1024]{2,0,1:T(8,128)(2,1)}), bf16[128,8,1024]{2,0,1:T(8,128)(2,1)}, u32[]{:S(2)}, u32[]{:S(2)}) async-start(bf16[128,8,1024]{2,0,1:T(8,128)(2,1)} %bitcast.198), calls=%async_computation.1 | async-start | bytes 4194304 | tf_op jit(solution)/shard_map/all_to_all | solution.py:55
  106.4 43.6 %all-to-all-done.1 = bf16[128,8,1024]{2,0,1:T(8,128)(2,1)} async-done(((bf16[128,8,1024]{2,0,1:T(8,128)(2,1)}), bf16[128,8,1024]{2,0,1:T(8,128)(2,1)}, u32[]{:S(2)}, u32[]{:S(2)}) %all-to-all-start.1) | async-done | bytes 2097184 | tf_op jit(solution)/shard_map/all_to_all | solution.py:55
  150.0 71.9 %while.41 = (s32[]{:T(128)}, f32[1024,512]{1,0:T(8,128)S(1)}, f32[1024]{0:T(1024)S(1)}, s32[]{:T(128)}, f32[]{:T(128)}, /*index=5*/f32[4,256,512]{2,1,0:T(8,128)...) while((s32[]{:T(128)}, f32[1024,512]{1,0:T(8,128)S(1)}, ...), condition=%wide.region_5.6_spmd.clone.clone, body=%wide.region_0.5_spmd.clone.sunk.clone | while | flops 3765605120 | bytes 20514200 | solution.py:122
  151.2 1.6 fusion.100
  152.8 1.4 fusion.101
  155.4 1.3 fusion.99
  156.6 1.2 multiply_reduce_fusion.4
  159.2 1.5 fusion.102
  160.8 3.1 fusion.103
  163.8 2.7 multiply_add_fusion.17
  169.1 1.6 fusion.100
  170.7 1.4 fusion.101
  173.4 1.3 fusion.99
  174.6 1.2 multiply_reduce_fusion.4
  177.2 1.5 fusion.102
  178.7 3.1 fusion.103
  181.8 2.7 multiply_add_fusion.17
  187.1 1.6 fusion.100
  188.7 1.4 fusion.101
  191.3 1.3 fusion.99
  195.1 1.5 fusion.102
  196.7 3.1 fusion.103
  199.8 2.7 multiply_add_fusion.17
  205.1 1.6 fusion.100
  206.7 1.4 fusion.101
  209.3 1.3 fusion.99
  213.1 1.5 fusion.102
  214.7 3.1 fusion.103
  217.8 2.7 multiply_add_fusion.17
  222.5 1.6 broadcast.103
  224.1 153.8 %while.40 = (s32[]{:T(128)}, f32[1024,512]{1,0:T(8,128)}, f32[1024]{0:T(1024)S(1)}, f32[1]{0:T(128)}, f32[1]{0:T(128)}, /*index=5*/pred[1]{0:T(512)(128)(4,1)}, ...) while((s32[]{:T(128)}, f32[1024,512]{1,0:T(8,128)}, ...), condition=%wide.region_7.8_spmd.clone, body=%wide.region_6.7_spmd.sunk.clone | while | flops 1050634 | bytes 14709080 | solution.py:139
  224.1 3.4 multiply_add_fusion.15
  227.5 4.5 collective-permute-start
  231.9 1.8 collective-permute-start.1
  233.7 41.3 %collective-permute-start.2 = (f32[1]{0:T(128)}, f32[1]{0:T(128)}, u32[]{:S(2)}, u32[]{:S(2)}) collective-permute-start(f32[1]{0:T(128)} %select_n.44), channel_id=1, source_target_pairs={{0,8},{8,16},{16,24},{1,9},{9,17},{17,25},{2,10},{10,18},{18,26},{... | collective-permute-start | bytes 20 | tf_op jit(solution)/shard_map/while/body/eval_jaxpr/ppermute | solution.py:17
  275.6 3.4 multiply_add_fusion.15
  279.0 5.5 %collective-permute-start = (f32[1024,512]{1,0:T(8,128)}, f32[1024,512]{1,0:T(8,128)}, u32[]{:S(2)}, u32[]{:S(2)}) collective-permute-start(f32[1024,512]{1,0:T(8,128)} %multiply_add_fusion.15), channel_id=1, source_target_pairs={{0,8},{8,16},{16,24},{1,9},{9,17},{17,25},{2,10},{10,18},{18,26},{... | collective-permute-start | bytes 6291464 | tf_op jit(solution)/shard_map/while/body/eval_jaxpr/ppermute | solution.py:17
  284.5 2.7 collective-permute-start.1
  287.2 39.4 %collective-permute-start.2 = (f32[1]{0:T(128)}, f32[1]{0:T(128)}, u32[]{:S(2)}, u32[]{:S(2)}) collective-permute-start(f32[1]{0:T(128)} %select_n.44), channel_id=1, source_target_pairs={{0,8},{8,16},{16,24},{1,9},{9,17},{17,25},{2,10},{10,18},{18,26},{... | collective-permute-start | bytes 20 | tf_op jit(solution)/shard_map/while/body/eval_jaxpr/ppermute | solution.py:17
  327.3 3.4 multiply_add_fusion.15
  330.6 5.5 %collective-permute-start = (f32[1024,512]{1,0:T(8,128)}, f32[1024,512]{1,0:T(8,128)}, u32[]{:S(2)}, u32[]{:S(2)}) collective-permute-start(f32[1024,512]{1,0:T(8,128)} %multiply_add_fusion.15), channel_id=1, source_target_pairs={{0,8},{8,16},{16,24},{1,9},{9,17},{17,25},{2,10},{10,18},{18,26},{... | collective-permute-start | bytes 6291464 | tf_op jit(solution)/shard_map/while/body/eval_jaxpr/ppermute | solution.py:17
  336.2 3.6 collective-permute-start.1
  339.7 37.5 %collective-permute-start.2 = (f32[1]{0:T(128)}, f32[1]{0:T(128)}, u32[]{:S(2)}, u32[]{:S(2)}) collective-permute-start(f32[1]{0:T(128)} %select_n.44), channel_id=1, source_target_pairs={{0,8},{8,16},{16,24},{1,9},{9,17},{17,25},{2,10},{10,18},{18,26},{... | collective-permute-start | bytes 20 | tf_op jit(solution)/shard_map/while/body/eval_jaxpr/ppermute | solution.py:17
  377.9 3.0 copy.30
  381.0 1.7 fusion.58
  382.7 8.4 %fusion.53 = bf16[1024,1,512]{0,2,1:T(8,128)(2,1)S(1)} fusion(f32[1024,512]{0,1:T(8,128)S(1)} %copy-done.5, f32[1024,512]{1,0:T(8,128)} %get-tuple-element.194, bf16[1024,1024]{1,0:T(8,128)(2,1)S(1)} %bitcast.194, f32[1024]{0:T(1024)S(1)} %abs_maximum_fusion, f32[1024]{0:T(1024)S(1)} %bitcast.228), kind=kOutput, calls=%fused_computation.67 | convolution fusion | flops 6444548096 | bytes 7348224 | tf_op jit(solution)/shard_map/dot_general | solution.py:144
  391.6 1.4 reduce.14
  394.4 33.2 %all_to_all.63 = bf16[8,2,32768]{2,1,0:T(2,128)(2,1)S(1)} all-to-all(bf16[8,2,32768]{2,1,0:T(2,128)(2,1)S(1)} %reshape.234), channel_id=1, replica_groups=mesh['seq'=4,'tensor'=8] {'tensor'}, dimensions={0} | all-to-all | bytes 2097152 | tf_op jit(solution)/shard_map/all_to_all | solution.py:147
  428.7 2.2 convert_bitcast_fusion
  432.1 3.0 copy.36
  435.1 3.1 fusion.56
  438.3 15.2 %multiply_reduce_fusion.1 = f32[128,8]{0,1:T(8,128)S(1)} fusion(f32[128,8]{0,1:T(8,128)S(1)} %bitcast.223, bf16[8,128,1,512]{3,2,1,0:T(2,128)(2,1)S(1)} %bitcast.196), kind=kLoop, calls=%fused_computation.65 | loop fusion | flops 2096128 | bytes 1056768 | tf_op jit(solution)/shard_map/reduce_sum | solution.py:157
  454.0 1.6 copy.38
  456.0 1.7 copy.37
  457.9 1.8 fusion.52
  (134 shorter events, 20.2 us)
Async XLA Ops:
  1.3 8.2 %all-to-all-start = ((bf16[128,8,2]{0,2,1:T(2,128)(2,1)}), bf16[128,8,2]{0,2,1:T(2,128)(2,1)S(1)}, u32[]{:S(2)}, u32[]{:S(2)}) async-start(bf16[128,8,2]{0,2,1:T(2,128)(2,1)} %bitcast.4), calls=%async_computation | async-start | bytes 8192 | tf_op jit(solution)/shard_map/all_to_all | solution.py:57
  6.8 9.0 %copy-start.6 = (bf16[128,4096]{1,0:T(8,128)(2,1)S(1)}, bf16[128,4096]{1,0:T(8,128)(2,1)}, u32[]{:S(2)}) copy-start(bf16[128,4096]{1,0:T(8,128)(2,1)} %param.12) | copy-start | bytes 3145732
  9.5 29.2 %all-to-all-start.2 = ((bf16[128,8,512]{2,0,1:T(8,128)(2,1)}), bf16[128,8,512]{2,0,1:T(8,128)(2,1)S(1)}, u32[]{:S(2)}, u32[]{:S(2)}) async-start(bf16[128,8,512]{2,0,1:T(8,128)(2,1)} %bitcast.127), calls=%async_computation.2 | async-start | bytes 2097152 | tf_op jit(solution)/shard_map/all_to_all | solution.py:56
  40.3 52.6 %all-to-all-start.3 = ((bf16[128,8,1024]{2,0,1:T(8,128)(2,1)}), bf16[128,8,1024]{2,0,1:T(8,128)(2,1)S(1)}, u32[]{:S(2)}, u32[]{:S(2)}) async-start(bf16[128,8,1024]{2,0,1:T(8,128)(2,1)} %bitcast.199), calls=%async_computation.3 | async-start | bytes 4194304 | tf_op jit(solution)/shard_map/all_to_all | solution.py:54
  92.9 3.6 copy-start
  96.5 8.2 %copy-start.9 = (s32[1024]{0:T(1024)S(1)}, s32[1024]{0:T(1024)}, u32[]{:S(2)}) copy-start(s32[1024]{0:T(1024)} %param.17) | copy-start | bytes 12292
  96.5 53.5 %all-to-all-start.1 = ((bf16[128,8,1024]{2,0,1:T(8,128)(2,1)}), bf16[128,8,1024]{2,0,1:T(8,128)(2,1)}, u32[]{:S(2)}, u32[]{:S(2)}) async-start(bf16[128,8,1024]{2,0,1:T(8,128)(2,1)} %bitcast.198), calls=%async_computation.1 | async-start | bytes 4194304 | tf_op jit(solution)/shard_map/all_to_all | solution.py:55
  150.0 2.8 copy-start.2
  163.8 3.4 copy-start.3
  167.9 2.8 copy-start.2
  181.8 3.4 copy-start.3
  185.9 2.8 copy-start.2
  199.8 3.4 copy-start.3
  203.9 2.8 copy-start.2
  217.8 3.4 copy-start.3
  227.5 47.5 %collective-permute-start = (f32[1024,512]{1,0:T(8,128)}, f32[1024,512]{1,0:T(8,128)}, u32[]{:S(2)}, u32[]{:S(2)}) collective-permute-start(f32[1024,512]{1,0:T(8,128)} %multiply_add_fusion.15), channel_id=1, source_target_pairs={{0,8},{8,16},{16,24},{1,9},{9,17},{17,25},{2,10},{10,18},{18,26},{... | collective-permute-start | bytes 6291464 | tf_op jit(solution)/shard_map/while/body/eval_jaxpr/ppermute | solution.py:17
  231.9 43.1 %collective-permute-start.1 = (f32[1024]{0:T(1024)S(1)}, f32[1024]{0:T(1024)S(1)}, u32[]{:S(2)}, u32[]{:S(2)}) collective-permute-start(f32[1024]{0:T(1024)S(1)} %multiply_add_fusion.16), channel_id=1, source_target_pairs={{0,8},{8,16},{16,24},{1,9},{9,17},{17,25},{2,10},{10,18},{18,26},{... | collective-permute-start | bytes 12296 | tf_op jit(solution)/shard_map/while/body/eval_jaxpr/ppermute | solution.py:17
  233.7 41.3 %collective-permute-start.2 = (f32[1]{0:T(128)}, f32[1]{0:T(128)}, u32[]{:S(2)}, u32[]{:S(2)}) collective-permute-start(f32[1]{0:T(128)} %select_n.44), channel_id=1, source_target_pairs={{0,8},{8,16},{16,24},{1,9},{9,17},{17,25},{2,10},{10,18},{18,26},{... | collective-permute-start | bytes 20 | tf_op jit(solution)/shard_map/while/body/eval_jaxpr/ppermute | solution.py:17
  279.0 47.6 %collective-permute-start = (f32[1024,512]{1,0:T(8,128)}, f32[1024,512]{1,0:T(8,128)}, u32[]{:S(2)}, u32[]{:S(2)}) collective-permute-start(f32[1024,512]{1,0:T(8,128)} %multiply_add_fusion.15), channel_id=1, source_target_pairs={{0,8},{8,16},{16,24},{1,9},{9,17},{17,25},{2,10},{10,18},{18,26},{... | collective-permute-start | bytes 6291464 | tf_op jit(solution)/shard_map/while/body/eval_jaxpr/ppermute | solution.py:17
  284.5 42.1 %collective-permute-start.1 = (f32[1024]{0:T(1024)S(1)}, f32[1024]{0:T(1024)S(1)}, u32[]{:S(2)}, u32[]{:S(2)}) collective-permute-start(f32[1024]{0:T(1024)S(1)} %multiply_add_fusion.16), channel_id=1, source_target_pairs={{0,8},{8,16},{16,24},{1,9},{9,17},{17,25},{2,10},{10,18},{18,26},{... | collective-permute-start | bytes 12296 | tf_op jit(solution)/shard_map/while/body/eval_jaxpr/ppermute | solution.py:17
  287.2 39.4 %collective-permute-start.2 = (f32[1]{0:T(128)}, f32[1]{0:T(128)}, u32[]{:S(2)}, u32[]{:S(2)}) collective-permute-start(f32[1]{0:T(128)} %select_n.44), channel_id=1, source_target_pairs={{0,8},{8,16},{16,24},{1,9},{9,17},{17,25},{2,10},{10,18},{18,26},{... | collective-permute-start | bytes 20 | tf_op jit(solution)/shard_map/while/body/eval_jaxpr/ppermute | solution.py:17
  330.6 46.6 %collective-permute-start = (f32[1024,512]{1,0:T(8,128)}, f32[1024,512]{1,0:T(8,128)}, u32[]{:S(2)}, u32[]{:S(2)}) collective-permute-start(f32[1024,512]{1,0:T(8,128)} %multiply_add_fusion.15), channel_id=1, source_target_pairs={{0,8},{8,16},{16,24},{1,9},{9,17},{17,25},{2,10},{10,18},{18,26},{... | collective-permute-start | bytes 6291464 | tf_op jit(solution)/shard_map/while/body/eval_jaxpr/ppermute | solution.py:17
  336.2 41.1 %collective-permute-start.1 = (f32[1024]{0:T(1024)S(1)}, f32[1024]{0:T(1024)S(1)}, u32[]{:S(2)}, u32[]{:S(2)}) collective-permute-start(f32[1024]{0:T(1024)S(1)} %multiply_add_fusion.16), channel_id=1, source_target_pairs={{0,8},{8,16},{16,24},{1,9},{9,17},{17,25},{2,10},{10,18},{18,26},{... | collective-permute-start | bytes 12296 | tf_op jit(solution)/shard_map/while/body/eval_jaxpr/ppermute | solution.py:17
  339.7 37.5 %collective-permute-start.2 = (f32[1]{0:T(128)}, f32[1]{0:T(128)}, u32[]{:S(2)}, u32[]{:S(2)}) collective-permute-start(f32[1]{0:T(128)} %select_n.44), channel_id=1, source_target_pairs={{0,8},{8,16},{16,24},{1,9},{9,17},{17,25},{2,10},{10,18},{18,26},{... | collective-permute-start | bytes 20 | tf_op jit(solution)/shard_map/while/body/eval_jaxpr/ppermute | solution.py:17
  377.9 3.1 copy-start.1
  381.0 1.7 copy-start.5
  456.0 1.7 copy-start.4
  456.0 1.8 copy-start.7
  456.0 1.8 copy-start.8
where the time goes:
time: 469 us; the launch traced here: 460 us
  starting transfers between devices  169 us (36%)
  waiting for transfers between devices  110 us (23%)
  matrix products  51.3 us (11%)
  other arithmetic  48.6 us (10%)
  local copies, waits for them, and re-layouts  33.3 us (7%)
  blocking collectives  33.2 us (7%)
  loops' own time  12.6 us (3%)
    ppermute x9, starting transfers between devices, shifted(): lax.ppermute(value, axis, [(source, source + steps) for source in range(i...  142 us
    all_to_all x1, waiting for transfers between devices, on_device(): lax.all_to_all(key_send, 'tensor', split_axis=1, concat_axis=0, tiled=True)  43.6 us
    all_to_all x1, waiting for transfers between devices, on_device(): lax.all_to_all(query_send, 'tensor', split_axis=1, concat_axis=0, tiled=T...  43 us
    all_to_all x1, blocking collectives, on_device(): lax.all_to_all(hidden.reshape(token_count, 1, column_count), 'tensor', sp...  33.2 us
    all_to_all x1, waiting for transfers between devices, on_device(): lax.all_to_all(value_send, 'tensor', split_axis=1, concat_axis=0, tiled=T...  22.7 us
    reduce_sum x2, other arithmetic, on_device(): variance = jnp.mean(centered * centered, axis=2, keepdims=True)  15.3 us
    dot_general x4, matrix products, span_step(): jnp.dot(query_float, cell_state, precision=precise)  12.3 us
    dot_general x4, matrix products, span_step(): jnp.dot(scaled_keys.T, value_f, precision=precise)  10.9 us
  transfers between devices with their start and end apart: 13, of which 4 were waited for; matrix products, arithmetic and copies ran while one was open for 1% of the time, Pallas kernels for 0%

commit v1 on v0

v1 whole, which is shorter than its diff:
```python
import functools
import math

import jax
import jax.numpy as jnp
from jax import lax
from jax.experimental import pallas as pl
from jax.experimental.pallas import tpu as pltpu
from jax.sharding import PartitionSpec as P

MESH = pl.DeviceIdType.MESH
F32 = jnp.float32
BF16 = jnp.bfloat16
EPS = 1e-05
TILE = 256
NONE = -1e30


def send(src, dst, send_sem, recv_sem, axis, index):
    return pltpu.make_async_remote_copy(
        src_ref=src,
        dst_ref=dst,
        send_sem=send_sem,
        recv_sem=recv_sem,
        device_id={axis: index},
        device_id_type=MESH,
    )


def kernel(
    dims,
    gates_ref,
    seg_ref,
    gain_ref,
    q_ref,
    k_ref,
    v_ref,
    og_ref,
    out_ref,
    gates_all,
    k_all,
    v_all,
    q_all,
    vt,
    lf_col,
    gate_col,
    cum_col,
    seg_col,
    tail_col,
    rows,
    meta,
    meta_all,
    tot,
    pre,
    pre_bf,
    stage,
    relay,
    tot_n,
    pre_n,
    stage_n,
    relay_n,
    num,
    qn,
    hid,
    out_rx,
    og_v,
    g_send,
    g_recv,
    k_send,
    k_fwd,
    k_recv,
    v_send,
    v_recv,
    q_send,
    q_fwd,
    q_recv,
    m_send,
    m_recv,
    r_send,
    r_recv,
    n_send,
    n_recv,
    o_send,
    o_recv,
    og_sem,
):
    seq_n, ten_n, heads, R, D = dims
    group = ten_n // heads
    C = D // group
    N = ten_n * R
    B = min(TILE, N)
    nb = N // B
    per = B // R
    chunk = min(256, D)
    nc = D // chunk
    levels = seq_n.bit_length() - 1
    scale = 1.0 / math.sqrt(D)
    t = lax.axis_index("tensor")
    s = lax.axis_index("seq")
    h = lax.div(t, group)
    m = lax.rem(t, group)

    def block(index):
        return pl.ds(pl.multiple_of(index * R, R), R)

    def tile(index):
        return pl.ds(pl.multiple_of(index * B, B), B)

    def head_cols(index):
        return pl.ds(pl.multiple_of(index * D, 128), D)

    def val_cols(index):
        return pl.ds(pl.multiple_of(index * C, 128), C)

    barrier = pltpu.get_barrier_semaphore()
    for d in range(1, ten_n):
        pl.semaphore_signal(
            barrier, inc=1, device_id={"tensor": lax.rem(t + d, ten_n)}, device_id_type=MESH
        )
    for d in range(1, seq_n):
        pl.semaphore_signal(
            barrier, inc=1, device_id={"seq": lax.rem(s + d, seq_n)}, device_id_type=MESH
        )
    pl.semaphore_wait(barrier, ten_n + seq_n - 2)

    def gate_copy(d):
        return send(
            gates_ref, gates_all.at[t], g_send.at[d - 1], g_recv.at[t], "tensor", lax.rem(t + d, ten_n)
        )

    def head_copy(src, dst, sem, rsem, d):
        hh = lax.rem(h + d, heads)
        return send(
            src.at[:, head_cols(hh)], dst.at[block(t)], sem.at[d - 1], rsem.at[t], "tensor", hh * group + m
        )

    def own_copy(src, dst, rsem):
        return pltpu.make_async_copy(src.at[:, head_cols(h)], dst.at[block(t)], rsem.at[t])

    def own_forward(src, dst, sem, rsem, g):
        return send(
            src.at[:, head_cols(h)],
            dst.at[block(t)],
            sem.at[g - 1],
            rsem.at[t],
            "tensor",
            h * group + lax.rem(m + g, group),
        )

    def source_block(d):
        return lax.rem(h + heads - d, heads) * group + m

    def forward(dst, sem, rsem, d, g):
        b = source_block(d)
        return send(
            dst.at[block(b)],
            dst.at[block(b)],
            sem.at[d * (group - 1) + g - 1],
            rsem.at[b],
            "tensor",
            h * group + lax.rem(m + g, group),
        )

    def arrive(dst, rsem, sem, b):
        send(dst.at[block(b)], dst.at[block(b)], sem.at[0], rsem.at[b], "tensor", lax.rem(t + 1, ten_n)).wait_recv()

    def val_copy(d):
        tt = lax.rem(t + d, ten_n)
        return send(
            v_ref.at[:, val_cols(tt)], v_all.at[block(t)], v_send.at[d - 1], v_recv.at[t], "tensor", tt
        )

    for d in range(1, ten_n):
        gate_copy(d).start()
    gates_all[t] = gates_ref[...]
    for d in range(1, heads):
        head_copy(k_ref, k_all, k_send, k_recv, d).start()
    own_copy(k_ref, k_all, k_recv).start()
    for g in range(1, group):
        own_forward(k_ref, k_all, k_fwd, k_recv, g).start()
    for d in range(1, ten_n):
        val_copy(d).start()
    own_val = pltpu.make_async_copy(v_ref.at[:, val_cols(t)], v_all.at[block(t)], v_recv.at[t])
    own_val.start()
    for d in range(1, heads):
        head_copy(q_ref, q_all, q_send, q_recv, d).start()
    own_copy(q_ref, q_all, q_recv).start()
    for g in range(1, group):
        own_forward(q_ref, q_all, q_fwd, q_recv, g).start()
    og_copy = pltpu.make_async_copy(og_ref, og_v, og_sem)
    og_copy.start()

    for d in range(1, ten_n):
        b = lax.rem(t + ten_n - d, ten_n)
        send(
            gates_ref, gates_all.at[b], g_send.at[0], g_recv.at[b], "tensor", lax.rem(t + 1, ten_n)
        ).wait_recv()
    eye_r = lax.broadcasted_iota(jnp.int32, (R, R), 0) == lax.broadcasted_iota(jnp.int32, (R, R), 1)

    def spread_gates(b, carry):
        both = gates_all[b]
        line = lax.broadcasted_iota(jnp.int32, both.shape, 0)
        gate_in = jnp.sum(jnp.where(line == h, both, 0.0), axis=0, keepdims=True)[:, :R]
        pre_f = jnp.sum(jnp.where(line == h + heads, both, 0.0), axis=0, keepdims=True)[:, :R]
        log_f = jnp.minimum(pre_f, 0.0) - jnp.log1p(jnp.exp(-jnp.abs(pre_f)))
        to_col = lambda row: jnp.broadcast_to(
            jnp.sum(jnp.where(eye_r, jnp.broadcast_to(row, (R, R)), 0.0), axis=1, keepdims=True), (R, 128)
        )
        lf_col[block(b)] = to_col(log_f)
        gate_col[block(b)] = to_col(gate_in)
        return carry

    lax.fori_loop(0, ten_n, spread_gates, 0)
    row_i = lax.broadcasted_iota(jnp.int32, (B, B), 0)
    col_i = lax.broadcasted_iota(jnp.int32, (B, B), 1)
    eye = row_i == col_i

    def as_row(mask, col):
        return jnp.sum(jnp.where(mask, jnp.broadcast_to(col, (B, B)), 0.0), axis=0, keepdims=True)

    def as_col(row):
        return jnp.broadcast_to(
            jnp.sum(jnp.where(eye, jnp.broadcast_to(row, (B, B)), 0.0), axis=1, keepdims=True), (B, 128)
        )

    total = jnp.zeros((1, 1), F32)
    for b in range(nb):
        here = pl.ds(b * B, B)
        cum = as_row(row_i <= col_i, lf_col[here, 0:1]) + total
        total = cum[:, B - 1 : B]
        rows[b, 0:1, :] = cum
        rows[b, 1:2, :] = as_row(eye, gate_col[here, 0:1]) - cum
        rows[b, 2:3, :] = seg_ref[b : b + 1, :]
        cum_col[here] = as_col(cum)
        seg_col[here] = as_col(seg_ref[b : b + 1, :])
    first_seg = seg_ref[0:1, 0:1]
    last_seg = seg_ref[nb - 1 : nb, B - 1 : B]
    for b in range(nb):
        here = pl.ds(b * B, B)
        kept = rows[b, 2:3, :] == last_seg
        tail = jnp.where(kept, jnp.exp(total + rows[b, 1:2, :]) * scale, 0.0)
        rows[b, 3:4, :] = tail
        tail_col[here] = as_col(tail)
    meta[0:1, :] = jnp.broadcast_to(total, (1, 128))
    meta[1:2, :] = jnp.broadcast_to(first_seg, (1, 128))
    meta[2:8, :] = jnp.broadcast_to(last_seg, (6, 128))

    def meta_copy(d):
        return send(
            meta, meta_all.at[s], m_send.at[d - 1], m_recv.at[s], "seq", lax.rem(s + d, seq_n)
        )

    for d in range(1, seq_n):
        meta_copy(d).start()
    meta_all[s] = meta[...]

    for d in range(1, heads):
        arrive(k_all, k_recv, k_send, source_block(d))
        for g in range(1, group):
            forward(k_all, k_fwd, k_recv, d, g).start()
    for d in range(1, ten_n):
        arrive(v_all, v_recv, v_send, lax.rem(t + ten_n - d, ten_n))
    own_val.wait()

    def scale_values(b, carry):
        vt[tile(b)] = (v_all[tile(b)].astype(F32) * tail_col[tile(b), 0:1]).astype(BF16)
        return carry

    lax.fori_loop(0, nb, scale_values, 0)
    own_copy(k_ref, k_all, k_recv).wait()
    for g in range(1, group):
        for hh in range(heads):
            arrive(k_all, k_recv, k_send, hh * group + lax.rem(m + g, group))

    def chunk_rows(c):
        return pl.ds(pl.multiple_of(c * chunk, chunk), chunk)

    def relay_copy(level, c):
        return send(
            stage.at[level, chunk_rows(c)],
            relay.at[level, chunk_rows(c)],
            r_send.at[level, c],
            r_recv.at[level, c],
            "seq",
            s + (1 - 2 * lax.rem(lax.div(s, 1 << level), 2)) * (1 << level),
        )

    def norm_copy(level):
        return send(
            stage_n.at[level],
            relay_n.at[level],
            n_send.at[level],
            n_recv.at[level],
            "seq",
            s + (1 - 2 * lax.rem(lax.div(s, 1 << level), 2)) * (1 << level),
        )

    def make_state(c, carry):
        part = lax.dot_general(
            k_all[:, pl.ds(pl.multiple_of(c * chunk, 128), chunk)],
            vt[...],
            (((0,), (0,)), ((), ())),
            preferred_element_type=F32,
        )
        tot[chunk_rows(c)] = part
        stage[0, chunk_rows(c)] = part.astype(BF16)
        relay_copy(0, c).start()
        return carry

    lax.fori_loop(0, nc, make_state, 0)
    tot_n[...] = jnp.zeros_like(tot_n)

    def add_norm(b, carry):
        tail = jnp.broadcast_to(rows[b][3:4, :], (16, B))
        line = lax.broadcasted_iota(jnp.int32, (16, B), 0)
        high = tail.astype(BF16).astype(F32)
        two = jnp.where(line == 0, high, jnp.where(line == 1, tail - high, 0.0)).astype(BF16)
        part = jnp.dot(two, k_all[tile(b)], preferred_element_type=F32)
        tot_n[...] += jnp.broadcast_to(part[0:1] + part[1:2], tot_n.shape)
        return carry

    lax.fori_loop(0, nb, add_norm, 0)
    stage_n[0] = tot_n[...]
    norm_copy(0).start()

    for d in range(1, seq_n):
        b = lax.rem(s + seq_n - d, seq_n)
        send(
            meta, meta_all.at[b], m_send.at[0], m_recv.at[b], "seq", lax.rem(s + 1, seq_n)
        ).wait_recv()

    def factors(level):
        width = 1 << level
        upper = lax.rem(lax.div(s, width), 2)
        base = lax.div(s, 2 * width) * (2 * width)
        low_end = base + width - 1
        high_end = base + 2 * width - 1
        to_here = jnp.zeros((1, 128), F32)
        to_end = jnp.zeros((1, 128), F32)
        for u in range(seq_n):
            log_u = meta_all[u][0:1, :]
            to_here = to_here + jnp.where((u > low_end) & (u < s), log_u, 0.0)
            to_end = to_end + jnp.where((u > low_end) & (u <= high_end), log_u, 0.0)
        low_last = meta_all[low_end][2:3, :]
        here = jnp.where(low_last == first_seg, jnp.exp(to_here), 0.0)
        end = jnp.where(low_last == meta_all[high_end][2:3, :], jnp.exp(to_end), 0.0)
        here = jnp.where(upper == 1, here, 0.0)[:, 0:1]
        own = jnp.where(upper == 1, 1.0, end)[:, 0:1]
        other = jnp.where(upper == 1, end, 1.0)[:, 0:1]
        return here, own, other

    def relay_level(level, between):
        here, own, other = factors(level)

        def join(c):
            relay_copy(level, c).wait_recv()
            got = relay[level, chunk_rows(c)].astype(F32)
            if level == 0:
                fresh = here * got
            else:
                fresh = pre[chunk_rows(c)] + here * got
            if level < levels - 1:
                pre[chunk_rows(c)] = fresh
                joined = own * tot[chunk_rows(c)] + other * got
                tot[chunk_rows(c)] = joined
                stage[level + 1, chunk_rows(c)] = joined.astype(BF16)
                relay_copy(level + 1, c).start()
            else:
                pre_bf[chunk_rows(c)] = fresh.astype(BF16)

        for c in range(nc):
            between(c)
            join(c)
        norm_copy(level).wait_recv()
        got = relay_n[level]
        if level == 0:
            pre_n[...] = here * got
        else:
            pre_n[...] = pre_n[...] + here * got
        if level < levels - 1:
            joined = own * tot_n[...] + other * got
            tot_n[...] = joined
            stage_n[level + 1] = joined
            norm_copy(level + 1).start()

    def take_query(d):
        if 1 <= d < heads:
            arrive(q_all, q_recv, q_send, source_block(d))
            for g in range(1, group):
                forward(q_all, q_fwd, q_recv, d, g).start()

    relay_level(0, lambda c: take_query(c))
    for d in range(nc, heads):
        take_query(d)
    own_copy(q_ref, q_all, q_recv).wait()
    for g in range(1, group):
        for hh in range(heads):
            arrive(q_all, q_recv, q_send, hh * group + lax.rem(m + g, group))

    def query_tile(i, carry):
        num[tile(i)] = jnp.zeros((B, C), F32)
        qn[tile(i)] = jnp.zeros((B, 128), F32)

        def key_tile(j, inner):
            scores = lax.dot_general(
                q_all[tile(i)], k_all[tile(j)], (((1,), (1,)), ((), ())), preferred_element_type=F32
            )
            row = rows[j]
            allowed = (i * B + row_i >= j * B + col_i) & (seg_col[tile(i), 0:1] == row[2:3, :])
            exponent = jnp.where(allowed, cum_col[tile(i), 0:1] + row[1:2, :], NONE)
            weighted = jnp.exp(exponent) * (scores * scale)
            qn[tile(i)] += jnp.broadcast_to(jnp.sum(weighted, axis=1, keepdims=True), (B, 128))
            num[tile(i)] += jnp.dot(weighted.astype(BF16), v_all[tile(j)], preferred_element_type=F32)
            return inner

        return lax.fori_loop(0, i + 1, key_tile, carry)

    lax.fori_loop(0, nb, query_tile, 0)
    for level in range(1, levels):
        relay_level(level, lambda c: None)

    line = lax.broadcasted_iota(jnp.int32, (16, D), 0)
    norm_row = jnp.broadcast_to(pre_n[0:1, :], (16, D))
    norm_high = norm_row.astype(BF16).astype(F32)
    norm_two = jnp.where(
        line == 0, norm_high, jnp.where(line == 1, norm_row - norm_high, 0.0)
    ).astype(BF16)
    pre_two = norm_two
    my_tile = lax.div(t, per)

    def out_copy(b):
        return send(hid.at[block(b)], out_rx.at[t], o_send.at[b], o_recv.at[t], "tensor", b)

    def own_out():
        return pltpu.make_async_copy(hid.at[block(t)], out_rx.at[t], o_recv.at[t])

    def finish_tile(step, carry):
        i = lax.rem(my_tile + 1 + step, nb)
        query = q_all[tile(i)]
        entry = jnp.where(
            seg_col[tile(i), 0:1] == first_seg, jnp.exp(cum_col[tile(i), 0:1]), 0.0
        )
        carried = jnp.dot(query, pre_bf[...], preferred_element_type=F32)
        carried_n = jnp.sum(
            lax.dot_general(query, pre_two, (((1,), (1,)), ((), ())), preferred_element_type=F32),
            axis=1,
            keepdims=True,
        )
        bottom = qn[tile(i), 0:1] + entry * carried_n
        top = num[tile(i)] + entry * carried
        hid[tile(i)] = (top / jnp.maximum(jnp.abs(bottom), 1.0)).astype(BF16)
        for p in range(per):
            b = i * per + p

            @pl.when(b != t)
            def _():
                out_copy(b).start()

            @pl.when(b == t)
            def _():
                own_out().start()

        return carry

    lax.fori_loop(0, nb, finish_tile, 0)

    og_copy.wait()
    own_out().wait()

    def finish_head(step, carry):
        hh = lax.rem(h + step, heads)
        parts = []
        for g in range(group):
            b = hh * group + g

            @pl.when(b != t)
            def _():
                send(
                    hid.at[block(b)], out_rx.at[b], o_send.at[b], o_recv.at[b], "tensor", lax.rem(t + 1, ten_n)
                ).wait_recv()

            parts.append(out_rx[b].astype(F32))
        mean = sum(jnp.sum(x, axis=1, keepdims=True) for x in parts) * (1.0 / D)
        parts = [x - mean for x in parts]
        var = sum(jnp.sum(x * x, axis=1, keepdims=True) for x in parts) * (1.0 / D)
        inv = lax.rsqrt(var + EPS)
        for g in range(group):
            cols = val_cols(hh * group + g)
            gate = og_v[:, cols].astype(F32)
            silu = gate / (1.0 + jnp.exp(-gate))
            out_ref[:, cols] = (parts[g] * inv * gain_ref[:, cols] * silu).astype(BF16)
        return carry

    lax.fori_loop(0, heads, finish_head, 0)

    for d in range(1, ten_n):
        gate_copy(d).wait_send()
        val_copy(d).wait_send()
        out_copy(lax.rem(t + d, ten_n)).wait_send()
    for d in range(1, heads):
        head_copy(k_ref, k_all, k_send, k_recv, d).wait_send()
        head_copy(q_ref, q_all, q_send, q_recv, d).wait_send()
    for g in range(1, group):
        own_forward(k_ref, k_all, k_fwd, k_recv, g).wait_send()
        own_forward(q_ref, q_all, q_fwd, q_recv, g).wait_send()
        for d in range(1, heads):
            forward(k_all, k_fwd, k_recv, d, g).wait_send()
            forward(q_all, q_fwd, q_recv, d, g).wait_send()
    for d in range(1, seq_n):
        meta_copy(d).wait_send()
    for level in range(levels):
        norm_copy(level).wait_send()
        for c in range(nc):
            relay_copy(level, c).wait_send()


def on_device(
    seq_n, ten_n, queries, key_rows, values, input_gate, forget_gate, segment_ids, output_gate, norm_gain
):
    R, inner = queries.shape
    heads = input_gate.shape[1]
    D = inner // heads
    group = ten_n // heads
    C = D // group
    N = ten_n * R
    B = min(TILE, N)
    nb = N // B
    nc = D // min(256, D)
    levels = seq_n.bit_length() - 1
    gates = jnp.concatenate([input_gate, forget_gate], axis=1).astype(F32).T
    lanes = max(R, 128)
    gates = jnp.pad(gates, ((0, -(2 * heads) % 8), (0, lanes - R)))
    lines = gates.shape[0]
    segs = segment_ids.astype(F32).reshape(nb, B)
    dma = pltpu.SemaphoreType.DMA
    vmem = pltpu.VMEM
    whole = pl.BlockSpec(memory_space=pltpu.VMEM)
    far = pl.BlockSpec(memory_space=pl.ANY)
    forwards = max(1, heads * (group - 1))
    return pl.pallas_call(
        functools.partial(kernel, (seq_n, ten_n, heads, R, D)),
        out_shape=jax.ShapeDtypeStruct((R, inner), BF16),
        in_specs=[whole, whole, whole, far, far, far, far],
        out_specs=whole,
        scratch_shapes=[
            vmem((ten_n, lines, lanes), F32),
            vmem((N, D), BF16),
            vmem((N, C), BF16),
            vmem((N, D), BF16),
            vmem((N, C), BF16),
            vmem((N, 128), F32),
            vmem((N, 128), F32),
            vmem((N, 128), F32),
            vmem((N, 128), F32),
            vmem((N, 128), F32),
            vmem((nb, 8, B), F32),
            vmem((8, 128), F32),
            vmem((seq_n, 8, 128), F32),
            vmem((D, C), F32),
            vmem((D, C), F32),
            vmem((D, C), BF16),
            vmem((levels, D, C), BF16),
            vmem((levels, D, C), BF16),
            vmem((8, D), F32),
            vmem((8, D), F32),
            vmem((levels, 8, D), F32),
            vmem((levels, 8, D), F32),
            vmem((N, C), F32),
            vmem((N, 128), F32),
            vmem((N, C), BF16),
            vmem((ten_n, R, C), BF16),
            vmem((R, inner), BF16),
            dma((ten_n,)),
            dma((ten_n,)),
            dma((heads,)),
            dma((forwards,)),
            dma((ten_n,)),
            dma((ten_n,)),
            dma((ten_n,)),
            dma((heads,)),
            dma((forwards,)),
            dma((ten_n,)),
            dma((seq_n,)),
            dma((seq_n,)),
            dma((levels, nc)),
            dma((levels, nc)),
            dma((levels,)),
            dma((levels,)),
            dma((ten_n,)),
            dma((ten_n,)),
            dma,
        ],
        compiler_params=pltpu.CompilerParams(
            collective_id=0, has_side_effects=True, vmem_limit_bytes=48 * 1024 * 1024
        ),
        cost_estimate=pl.CostEstimate(
            flops=2 * N * (N * D + N * C + 2 * D * C), bytes_accessed=10 * R * inner, transcendentals=N * N
        ),
    )(gates, segs, norm_gain.reshape(1, inner), queries, key_rows, values, output_gate)


def solution(mesh):
    rows = P(("seq", "tensor"), None)
    return jax.shard_map(
        functools.partial(on_device, mesh.shape["seq"], mesh.shape["tensor"]),
        mesh=mesh,
        in_specs=(rows, rows, rows, rows, rows, P("seq"), rows, P()),
        out_specs=rows,
        check_vma=False,
    )
```

time: 469 us -> 127 us (0.27)
  the two profiles are of different devices: /device:TPU:17 before, /device:TPU:25 now
where the time goes in v1:
time: 127 us; the launch traced here: 126 us
  Pallas kernels  119 us (94%)
  local copies, waits for them, and re-layouts  5.88 us (5%)
  other arithmetic  1.4 us (1%)
    pallas_call x1, Pallas kernels, on_device(): pl.pallas_call(functools.partial(kernel, (seq_n, ten_n, heads, R, D)), ou...  119 us
    unnamed x11, local copies, waits for them, and re-layouts  5.87 us

profile of v1, /device:TPU:25, one launch (start us, length us, event | category | flops | bytes accessed | tf_op | source)
XLA Modules:
  0.0 126.2 jit_solution(159914398900202076)
XLA Ops:
  0.0 0.0 copy-start.4
  0.0 0.7 convert_bitcast_fusion.gates_ref
  0.7 0.7 convert_element_type.4
  1.4 0.0 copy-done.4
  1.4 0.0 copy-start
  1.4 1.2 copy-done
  2.6 0.0 copy-start.1
  2.6 1.2 copy-done.1
  3.9 0.0 copy-start.2
  3.9 1.2 copy-done.2
  5.1 0.0 copy-start.3
  5.1 1.2 copy-done.3
  6.3 118.9 %shard_map.82 = bf16[128,4096]{1,0:T(8,128)(2,1)S(1)} custom-call(f32[8,128]{1,0:T(8,128)S(1)} %convert_bitcast_fusion.gates_ref, f32[4,256]{1,0:T(4,128)S(1)} %reshape.6.seg_ref, f32[1,4096]{1,0:T(1,128)S(1)} %bitcast.3, bf16[128,4096]{1,0:T(8,128)(2,1)S(1)} %copy-done, bf16[128,4096]{1,0:T(8,128)(2,1)S(1)} %copy-done.1, bf16[128,4096]{1,0:T(8,128)(2,1)S(1)} %copy-done.2, ...), custom_call_target="tpu_custom_call" | custom-call | flops 5368709120 | bytes 5242880 | tf_op jit(solution)/shard_map/pallas_call | solution.py:540
  125.2 1.0 copy.10
  (1 shorter events, 0.0 us)
Async XLA Ops:
  0.0 1.4 %copy-start.4 = (f32[4096]{0:T(1024)S(1)}, f32[4096]{0:T(1024)}, u32[]{:S(2)}) copy-start(f32[4096]{0:T(1024)} %param.15) | copy-start | bytes 49156
  1.4 1.2 copy-start
  2.6 1.2 copy-start.1
  3.9 1.2 copy-start.2
  5.1 1.2 copy-start.3

commit v2 on v1

--- a/solution.py
+++ b/solution.py
@@ -12,7 +12,6 @@
 F32 = jnp.float32
 BF16 = jnp.bfloat16
 EPS = 1e-05
-TILE = 256
 NONE = -1e30
 
 
@@ -83,14 +82,14 @@
     o_send,
     o_recv,
     og_sem,
+    k_own,
 ):
     seq_n, ten_n, heads, R, D = dims
     group = ten_n // heads
     C = D // group
     N = ten_n * R
-    B = min(TILE, N)
-    nb = N // B
-    per = B // R
+    B = group * R
+    nb = heads
     chunk = min(256, D)
     nc = D // chunk
     levels = seq_n.bit_length() - 1
@@ -164,6 +163,41 @@
     def arrive(dst, rsem, sem, b):
         send(dst.at[block(b)], dst.at[block(b)], sem.at[0], rsem.at[b], "tensor", lax.rem(t + 1, ten_n)).wait_recv()
 
+    def key_copy(d, c):
+        hh = lax.rem(h + d, heads)
+        return send(
+            k_ref.at[:, pl.ds(pl.multiple_of(hh * D + c * chunk, 128), chunk)],
+            k_all.at[block(t), pl.ds(c * chunk, chunk)],
+            k_send.at[d - 1, c],
+            k_recv.at[t, c],
+            "tensor",
+            hh * group + m,
+        )
+
+    def key_forward(d, g, c):
+        b = source_block(d)
+        here = k_all.at[block(b), pl.ds(c * chunk, chunk)]
+        source = k_ref.at[:, pl.ds(pl.multiple_of(h * D + c * chunk, 128), chunk)] if d == 0 else here
+        return send(
+            source,
+            here,
+            k_fwd.at[d * (group - 1) + g - 1, c],
+            k_recv.at[b, c],
+            "tensor",
+            h * group + lax.rem(m + g, group),
+        )
+
+    def key_arrive(b, c):
+        here = k_all.at[block(b), pl.ds(c * chunk, chunk)]
+        send(here, here, k_send.at[0, c], k_recv.at[b, c], "tensor", lax.rem(t + 1, ten_n)).wait_recv()
+
+    def send_keys(c):
+        for d in range(1, heads):
+            key_copy(d, c).start()
+
+    def send_queries(d):
+        head_copy(q_ref, q_all, q_send, q_recv, d).start()
+
     def val_copy(d):
         tt = lax.rem(t + d, ten_n)
         return send(
@@ -173,20 +207,26 @@
     for d in range(1, ten_n):
         gate_copy(d).start()
     gates_all[t] = gates_ref[...]
-    for d in range(1, heads):
-        head_copy(k_ref, k_all, k_send, k_recv, d).start()
-    own_copy(k_ref, k_all, k_recv).start()
-    for g in range(1, group):
-        own_forward(k_ref, k_all, k_fwd, k_recv, g).start()
     for d in range(1, ten_n):
         val_copy(d).start()
     own_val = pltpu.make_async_copy(v_ref.at[:, val_cols(t)], v_all.at[block(t)], v_recv.at[t])
     own_val.start()
-    for d in range(1, heads):
-        head_copy(q_ref, q_all, q_send, q_recv, d).start()
+    own_key = pltpu.make_async_copy(k_ref.at[:, head_cols(h)], k_all.at[block(t)], k_own)
+    own_key.start()
     own_copy(q_ref, q_all, q_recv).start()
     for g in range(1, group):
+        for c in range(nc):
+            key_forward(0, g, c).start()
         own_forward(q_ref, q_all, q_fwd, q_recv, g).start()
+    queue = [functools.partial(send_keys, c) for c in range(nc)]
+    queue += [functools.partial(send_queries, d) for d in range(1, heads)]
+
+    def next_piece():
+        if queue:
+            queue.pop(0)()
+
+    next_piece()
+    next_piece()
     og_copy = pltpu.make_async_copy(og_ref, og_v, og_sem)
     og_copy.start()
 
@@ -223,6 +263,9 @@
             jnp.sum(jnp.where(eye, jnp.broadcast_to(row, (B, B)), 0.0), axis=1, keepdims=True), (B, 128)
         )
 
+    def segs(b):
+        return seg_ref[0:1, b * B : (b + 1) * B].astype(F32)
+
     total = jnp.zeros((1, 1), F32)
     for b in range(nb):
         here = pl.ds(b * B, B)
@@ -230,11 +273,11 @@
         total = cum[:, B - 1 : B]
         rows[b, 0:1, :] = cum
         rows[b, 1:2, :] = as_row(eye, gate_col[here, 0:1]) - cum
-        rows[b, 2:3, :] = seg_ref[b : b + 1, :]
+        rows[b, 2:3, :] = segs(b)
         cum_col[here] = as_col(cum)
-        seg_col[here] = as_col(seg_ref[b : b + 1, :])
-    first_seg = seg_ref[0:1, 0:1]
-    last_seg = seg_ref[nb - 1 : nb, B - 1 : B]
+        seg_col[here] = as_col(segs(b))
+    first_seg = segs(0)[:, 0:1]
+    last_seg = segs(nb - 1)[:, B - 1 : B]
     for b in range(nb):
         here = pl.ds(b * B, B)
         kept = rows[b, 2:3, :] == last_seg
@@ -254,24 +297,16 @@
         meta_copy(d).start()
     meta_all[s] = meta[...]
 
-    for d in range(1, heads):
-        arrive(k_all, k_recv, k_send, source_block(d))
-        for g in range(1, group):
-            forward(k_all, k_fwd, k_recv, d, g).start()
     for d in range(1, ten_n):
         arrive(v_all, v_recv, v_send, lax.rem(t + ten_n - d, ten_n))
     own_val.wait()
+    next_piece()
 
     def scale_values(b, carry):
         vt[tile(b)] = (v_all[tile(b)].astype(F32) * tail_col[tile(b), 0:1]).astype(BF16)
         return carry
 
     lax.fori_loop(0, nb, scale_values, 0)
-    own_copy(k_ref, k_all, k_recv).wait()
-    for g in range(1, group):
-        for hh in range(heads):
-            arrive(k_all, k_recv, k_send, hh * group + lax.rem(m + g, group))
-
     def chunk_rows(c):
         return pl.ds(pl.multiple_of(c * chunk, chunk), chunk)
 
@@ -295,33 +330,13 @@
             s + (1 - 2 * lax.rem(lax.div(s, 1 << level), 2)) * (1 << level),
         )
 
-    def make_state(c, carry):
+    def make_state(c):
         part = lax.dot_general(
-            k_all[:, pl.ds(pl.multiple_of(c * chunk, 128), chunk)],
-            vt[...],
-            (((0,), (0,)), ((), ())),
-            preferred_element_type=F32,
+            k_all[:, pl.ds(c * chunk, chunk)], vt[...], (((0,), (0,)), ((), ())), preferred_element_type=F32
         )
         tot[chunk_rows(c)] = part
         stage[0, chunk_rows(c)] = part.astype(BF16)
         relay_copy(0, c).start()
-        return carry
-
-    lax.fori_loop(0, nc, make_state, 0)
-    tot_n[...] = jnp.zeros_like(tot_n)
-
-    def add_norm(b, carry):
-        tail = jnp.broadcast_to(rows[b][3:4, :], (16, B))
-        line = lax.broadcasted_iota(jnp.int32, (16, B), 0)
-        high = tail.astype(BF16).astype(F32)
-        two = jnp.where(line == 0, high, jnp.where(line == 1, tail - high, 0.0)).astype(BF16)
-        part = jnp.dot(two, k_all[tile(b)], preferred_element_type=F32)
-        tot_n[...] += jnp.broadcast_to(part[0:1] + part[1:2], tot_n.shape)
-        return carry
-
-    lax.fori_loop(0, nb, add_norm, 0)
-    stage_n[0] = tot_n[...]
-    norm_copy(0).start()
 
     for d in range(1, seq_n):
         b = lax.rem(s + seq_n - d, seq_n)
@@ -349,55 +364,44 @@
         other = jnp.where(upper == 1, end, 1.0)[:, 0:1]
         return here, own, other
 
-    def relay_level(level, between):
-        here, own, other = factors(level)
-
-        def join(c):
-            relay_copy(level, c).wait_recv()
-            got = relay[level, chunk_rows(c)].astype(F32)
-            if level == 0:
-                fresh = here * got
-            else:
-                fresh = pre[chunk_rows(c)] + here * got
-            if level < levels - 1:
-                pre[chunk_rows(c)] = fresh
-                joined = own * tot[chunk_rows(c)] + other * got
-                tot[chunk_rows(c)] = joined
-                stage[level + 1, chunk_rows(c)] = joined.astype(BF16)
-                relay_copy(level + 1, c).start()
-            else:
-                pre_bf[chunk_rows(c)] = fresh.astype(BF16)
-
-        for c in range(nc):
-            between(c)
-            join(c)
+    links = [factors(level) for level in range(levels)]
+
+    def join(level, c):
+        here, own, other = links[level]
+        relay_copy(level, c).wait_recv()
+        got = relay[level, chunk_rows(c)].astype(F32)
+        fresh = here * got
+        if level > 0:
+            fresh = pre[chunk_rows(c)] + fresh
+        if level < levels - 1:
+            pre[chunk_rows(c)] = fresh
+            joined = own * tot[chunk_rows(c)] + other * got
+            tot[chunk_rows(c)] = joined
+            stage[level + 1, chunk_rows(c)] = joined.astype(BF16)
+            relay_copy(level + 1, c).start()
+        else:
+            pre_bf[chunk_rows(c)] = fresh.astype(BF16)
+
+    def join_norm(level):
+        here, own, other = links[level]
         norm_copy(level).wait_recv()
         got = relay_n[level]
-        if level == 0:
-            pre_n[...] = here * got
-        else:
-            pre_n[...] = pre_n[...] + here * got
+        fresh = here * got
+        if level > 0:
+            fresh = pre_n[...] + fresh
+        pre_n[...] = fresh
         if level < levels - 1:
             joined = own * tot_n[...] + other * got
             tot_n[...] = joined
             stage_n[level + 1] = joined
             norm_copy(level + 1).start()
 
-    def take_query(d):
-        if 1 <= d < heads:
-            arrive(q_all, q_recv, q_send, source_block(d))
-            for g in range(1, group):
-                forward(q_all, q_fwd, q_recv, d, g).start()
-
-    relay_level(0, lambda c: take_query(c))
-    for d in range(nc, heads):
-        take_query(d)
-    own_copy(q_ref, q_all, q_recv).wait()
-    for g in range(1, group):
-        for hh in range(heads):
-            arrive(q_all, q_recv, q_send, hh * group + lax.rem(m + g, group))
-
-    def query_tile(i, carry):
+    def join_due(step):
+        for level in range(levels):
+            if 0 <= step - 1 - level < nc:
+                join(level, step - 1 - level)
+
+    def query_tile(i):
         num[tile(i)] = jnp.zeros((B, C), F32)
         qn[tile(i)] = jnp.zeros((B, 128), F32)
 
@@ -413,11 +417,60 @@
             num[tile(i)] += jnp.dot(weighted.astype(BF16), v_all[tile(j)], preferred_element_type=F32)
             return inner
 
-        return lax.fori_loop(0, i + 1, key_tile, carry)
-
-    lax.fori_loop(0, nb, query_tile, 0)
+        lax.fori_loop(0, i + 1, key_tile, 0)
+
+    def take_query(d):
+        arrive(q_all, q_recv, q_send, source_block(d))
+        for g in range(1, group):
+            forward(q_all, q_fwd, q_recv, d, g).start()
+
+    def take_others(d):
+        for g in range(1, group):
+            b = lax.rem(h + heads - d, heads) * group + lax.rem(m + g, group)
+            arrive(q_all, q_recv, q_send, b)
+
+    own_key.wait()
+    for c in range(nc):
+        for d in range(1, heads):
+            key_arrive(source_block(d), c)
+            for g in range(1, group):
+                key_forward(d, g, c).start()
+        next_piece()
+        for g in range(1, group):
+            for hh in range(heads):
+                key_arrive(hh * group + lax.rem(m + g, group), c)
+        make_state(c)
+        join_due(c)
+    while queue:
+        next_piece()
+    tot_n[...] = jnp.zeros_like(tot_n)
+
+    def add_norm(b, carry):
+        tail = jnp.broadcast_to(rows[b][3:4, :], (16, B))
+        line = lax.broadcasted_iota(jnp.int32, (16, B), 0)
+        high = tail.astype(BF16).astype(F32)
+        two = jnp.where(line == 0, high, jnp.where(line == 1, tail - high, 0.0)).astype(BF16)
+        part = jnp.dot(two, k_all[tile(b)], preferred_element_type=F32)
+        tot_n[...] += jnp.broadcast_to(part[0:1] + part[1:2], tot_n.shape)
+        return carry
+
+    lax.fori_loop(0, nb, add_norm, 0)
+    stage_n[0] = tot_n[...]
+    norm_copy(0).start()
+
+
+    own_copy(q_ref, q_all, q_recv).wait()
+    take_others(0)
+    query_tile(h)
+    join_due(nc)
+    join_norm(0)
+    take_query(1)
+    take_others(1)
+    query_tile(lax.rem(h + heads - 1, heads))
+    for step in range(nc + 1, nc + levels):
+        join_due(step)
     for level in range(1, levels):
-        relay_level(level, lambda c: None)
+        join_norm(level)
 
     line = lax.broadcasted_iota(jnp.int32, (16, D), 0)
     norm_row = jnp.broadcast_to(pre_n[0:1, :], (16, D))
@@ -425,8 +478,6 @@
     norm_two = jnp.where(
         line == 0, norm_high, jnp.where(line == 1, norm_row - norm_high, 0.0)
     ).astype(BF16)
-    pre_two = norm_two
-    my_tile = lax.div(t, per)
 
     def out_copy(b):
         return send(hid.at[block(b)], out_rx.at[t], o_send.at[b], o_recv.at[t], "tensor", b)
@@ -434,35 +485,35 @@
     def own_out():
         return pltpu.make_async_copy(hid.at[block(t)], out_rx.at[t], o_recv.at[t])
 
-    def finish_tile(step, carry):
-        i = lax.rem(my_tile + 1 + step, nb)
+    def finish_tile(d):
+        i = lax.rem(h + heads - d, heads)
         query = q_all[tile(i)]
         entry = jnp.where(
             seg_col[tile(i), 0:1] == first_seg, jnp.exp(cum_col[tile(i), 0:1]), 0.0
         )
         carried = jnp.dot(query, pre_bf[...], preferred_element_type=F32)
         carried_n = jnp.sum(
-            lax.dot_general(query, pre_two, (((1,), (1,)), ((), ())), preferred_element_type=F32),
+            lax.dot_general(query, norm_two, (((1,), (1,)), ((), ())), preferred_element_type=F32),
             axis=1,
             keepdims=True,
         )
         bottom = qn[tile(i), 0:1] + entry * carried_n
         top = num[tile(i)] + entry * carried
         hid[tile(i)] = (top / jnp.maximum(jnp.abs(bottom), 1.0)).astype(BF16)
-        for p in range(per):
-            b = i * per + p
-
-            @pl.when(b != t)
-            def _():
-                out_copy(b).start()
-
-            @pl.when(b == t)
-            def _():
-                own_out().start()
-
-        return carry
-
-    lax.fori_loop(0, nb, finish_tile, 0)
+        for g in range(1, group):
+            out_copy(i * group + lax.rem(m + g, group)).start()
+        if d == 0:
+            own_out().start()
+        else:
+            out_copy(i * group + m).start()
+
+    finish_tile(1)
+    finish_tile(0)
+    for d in range(2, heads):
+        take_query(d)
+        take_others(d)
+        query_tile(lax.rem(h + heads - d, heads))
+        finish_tile(d)
 
     og_copy.wait()
     own_out().wait()
@@ -498,13 +549,15 @@
         val_copy(d).wait_send()
         out_copy(lax.rem(t + d, ten_n)).wait_send()
     for d in range(1, heads):
-        head_copy(k_ref, k_all, k_send, k_recv, d).wait_send()
         head_copy(q_ref, q_all, q_send, q_recv, d).wait_send()
+        for c in range(nc):
+            key_copy(d, c).wait_send()
     for g in range(1, group):
-        own_forward(k_ref, k_all, k_fwd, k_recv, g).wait_send()
         own_forward(q_ref, q_all, q_fwd, q_recv, g).wait_send()
+        for c in range(nc):
+            for d in range(heads):
+                key_forward(d, g, c).wait_send()
         for d in range(1, heads):
-            forward(k_all, k_fwd, k_recv, d, g).wait_send()
             forward(q_all, q_fwd, q_recv, d, g).wait_send()
     for d in range(1, seq_n):
         meta_copy(d).wait_send()
@@ -523,19 +576,17 @@
     group = ten_n // heads
     C = D // group
     N = ten_n * R
-    B = min(TILE, N)
-    nb = N // B
     nc = D // min(256, D)
     levels = seq_n.bit_length() - 1
     gates = jnp.concatenate([input_gate, forget_gate], axis=1).astype(F32).T
     lanes = max(R, 128)
     gates = jnp.pad(gates, ((0, -(2 * heads) % 8), (0, lanes - R)))
     lines = gates.shape[0]
-    segs = segment_ids.astype(F32).reshape(nb, B)
+    segs = segment_ids.reshape(1, N)
     dma = pltpu.SemaphoreType.DMA
     vmem = pltpu.VMEM
     whole = pl.BlockSpec(memory_space=pltpu.VMEM)
-    far = pl.BlockSpec(memory_space=pl.ANY)
+    far = pl.BlockSpec(memory_space=pltpu.HBM)
     forwards = max(1, heads * (group - 1))
     return pl.pallas_call(
         functools.partial(kernel, (seq_n, ten_n, heads, R, D)),
@@ -553,7 +604,7 @@
             vmem((N, 128), F32),
             vmem((N, 128), F32),
             vmem((N, 128), F32),
-            vmem((nb, 8, B), F32),
+            vmem((heads, 8, group * R), F32),
             vmem((8, 128), F32),
             vmem((seq_n, 8, 128), F32),
             vmem((D, C), F32),
@@ -572,9 +623,9 @@
             vmem((R, inner), BF16),
             dma((ten_n,)),
             dma((ten_n,)),
-            dma((heads,)),
-            dma((forwards,)),
-            dma((ten_n,)),
+            dma((heads, nc)),
+            dma((forwards, nc)),
+            dma((ten_n, nc)),
             dma((ten_n,)),
             dma((ten_n,)),
             dma((heads,)),
@@ -589,6 +640,7 @@
             dma((ten_n,)),
             dma((ten_n,)),
             dma,
+            dma,
         ],
         compiler_params=pltpu.CompilerParams(
             collective_id=0, has_side_effects=True, vmem_limit_bytes=48 * 1024 * 1024

time: 127 us -> 113 us (0.89)
  the two profiles are of different devices: /device:TPU:25 before, /device:TPU:17 now
where the time goes in v2:
time: 113 us
  Pallas kernels  106 us (94%)
  local copies, waits for them, and re-layouts  7.29 us (6%)
    pallas_call x1, Pallas kernels, on_device(): pl.pallas_call(functools.partial(kernel, (seq_n, ten_n, heads, R, D)), ou...  106 us
    unnamed x17, local copies, waits for them, and re-layouts  7.29 us

profile of v2, /device:TPU:17, one launch (start us, length us, event | category | flops | bytes accessed | tf_op | source)
XLA Modules:
  0.0 112.9 jit_solution(6694320179616635874)
XLA Ops:
  0.0 0.0 copy-start.6
  0.0 0.0 copy-start.7
  0.0 0.0 copy-start.5
  0.0 0.7 copy-done.6
  0.7 0.0 copy-done.7
  0.7 0.0 copy-done.5
  0.7 0.0 copy-start
  0.7 1.2 %copy-done = bf16[128,4096]{1,0:T(8,128)(2,1)S(1)} copy-done((bf16[128,4096]{1,0:T(8,128)(2,1)S(1)}, bf16[128,4096]{1,0:T(8,128)(2,1)}, u32[]{:S(2)}) %copy-start) | copy-done | bytes 1048600
  1.9 0.0 copy-start.1
  1.9 1.2 %copy-done.1 = bf16[128,4096]{1,0:T(8,128)(2,1)S(1)} copy-done((bf16[128,4096]{1,0:T(8,128)(2,1)S(1)}, bf16[128,4096]{1,0:T(8,128)(2,1)}, u32[]{:S(2)}) %copy-start.1) | copy-done | bytes 1048600
  3.2 0.0 copy-start.2
  3.2 1.2 %copy-done.2 = bf16[128,4096]{1,0:T(8,128)(2,1)S(1)} copy-done((bf16[128,4096]{1,0:T(8,128)(2,1)S(1)}, bf16[128,4096]{1,0:T(8,128)(2,1)}, u32[]{:S(2)}) %copy-start.2) | copy-done | bytes 1048600
  4.4 0.0 copy-start.3
  4.4 1.2 %copy-done.3 = bf16[128,4096]{1,0:T(8,128)(2,1)S(1)} copy-done((bf16[128,4096]{1,0:T(8,128)(2,1)S(1)}, bf16[128,4096]{1,0:T(8,128)(2,1)}, u32[]{:S(2)}) %copy-start.3) | copy-done | bytes 1048600
  5.6 0.0 copy-start.4
  5.6 0.7 copy-done.4
  6.3 105.6 %shard_map.82 = bf16[128,4096]{1,0:T(8,128)(2,1)S(1)} custom-call(f32[8,128]{1,0:T(8,128)S(1)} %convert_bitcast_fusion.gates_ref, s32[1,1024]{1,0:T(1,128)S(1)} %bitcast.5, f32[1,4096]{1,0:T(1,128)S(1)} %bitcast.4, bf16[128,4096]{1,0:T(8,128)(2,1)S(1)} %copy-done, bf16[128,4096]{1,0:T(8,128)(2,1)S(1)} %copy-done.1, bf16[128,4096]{1,0:T(8,128)(2,1)S(1)} %copy-done.2, ...), custom_call_target="tpu_custom_call" | custom-call | flops 5368709120 | bytes 5242880 | tf_op jit(solution)/shard_map/pallas_call | solution.py:591
  111.9 1.0 copy.10
  (1 shorter events, 0.0 us)
Async XLA Ops:
  0.0 0.7 copy-start.6
  0.0 0.7 copy-start.7
  0.0 0.7 copy-start.5
  0.7 1.2 %copy-start = (bf16[128,4096]{1,0:T(8,128)(2,1)S(1)}, bf16[128,4096]{1,0:T(8,128)(2,1)}, u32[]{:S(2)}) copy-start(bf16[128,4096]{1,0:T(8,128)(2,1)} %q_ref.1) | copy-start | bytes 3145732
  1.9 1.2 %copy-start.1 = (bf16[128,4096]{1,0:T(8,128)(2,1)S(1)}, bf16[128,4096]{1,0:T(8,128)(2,1)}, u32[]{:S(2)}) copy-start(bf16[128,4096]{1,0:T(8,128)(2,1)} %k_ref.1) | copy-start | bytes 3145732
  3.2 1.2 %copy-start.2 = (bf16[128,4096]{1,0:T(8,128)(2,1)S(1)}, bf16[128,4096]{1,0:T(8,128)(2,1)}, u32[]{:S(2)}) copy-start(bf16[128,4096]{1,0:T(8,128)(2,1)} %v_ref.1) | copy-start | bytes 3145732
  4.4 1.2 %copy-start.3 = (bf16[128,4096]{1,0:T(8,128)(2,1)S(1)}, bf16[128,4096]{1,0:T(8,128)(2,1)}, u32[]{:S(2)}) copy-start(bf16[128,4096]{1,0:T(8,128)(2,1)} %og_ref.1) | copy-start | bytes 3145732
  5.6 0.7 copy-start.4

commit v3 on v2

--- a/solution.py
+++ b/solution.py
@@ -12,6 +12,7 @@
 F32 = jnp.float32
 BF16 = jnp.bfloat16
 EPS = 1e-05
+LIMIT = 63 * 1024 * 1024
 NONE = -1e30
 
 
@@ -28,7 +29,8 @@
 
 def kernel(
     dims,
-    gates_ref,
+    in_gate_ref,
+    forget_ref,
     seg_ref,
     gain_ref,
     q_ref,
@@ -36,6 +38,7 @@
     v_ref,
     og_ref,
     out_ref,
+    gates_ref,
     gates_all,
     k_all,
     v_all,
@@ -83,6 +86,8 @@
     o_recv,
     og_sem,
     k_own,
+    out_v,
+    w_sem,
 ):
     seq_n, ten_n, heads, R, D = dims
     group = ten_n // heads
@@ -111,6 +116,8 @@
     def val_cols(index):
         return pl.ds(pl.multiple_of(index * C, 128), C)
 
+    gates_ref[0:heads, 0:R] = in_gate_ref[...].astype(F32)
+    gates_ref[heads : 2 * heads, 0:R] = forget_ref[...].astype(F32)
     barrier = pltpu.get_barrier_semaphore()
     for d in range(1, ten_n):
         pl.semaphore_signal(
@@ -518,6 +525,11 @@
     og_copy.wait()
     own_out().wait()
 
+    def write_copy(hh):
+        return pltpu.make_async_copy(
+            out_v.at[:, head_cols(hh)], out_ref.at[:, head_cols(hh)], w_sem.at[hh]
+        )
+
     def finish_head(step, carry):
         hh = lax.rem(h + step, heads)
         parts = []
@@ -539,7 +551,8 @@
             cols = val_cols(hh * group + g)
             gate = og_v[:, cols].astype(F32)
             silu = gate / (1.0 + jnp.exp(-gate))
-            out_ref[:, cols] = (parts[g] * inv * gain_ref[:, cols] * silu).astype(BF16)
+            out_v[:, cols] = (parts[g] * inv * gain_ref[:, cols] * silu).astype(BF16)
+        write_copy(hh).start()
         return carry
 
     lax.fori_loop(0, heads, finish_head, 0)
@@ -561,6 +574,8 @@
             forward(q_all, q_fwd, q_recv, d, g).wait_send()
     for d in range(1, seq_n):
         meta_copy(d).wait_send()
+    for hh in range(heads):
+        write_copy(hh).wait()
     for level in range(levels):
         norm_copy(level).wait_send()
         for c in range(nc):
@@ -578,10 +593,8 @@
     N = ten_n * R
     nc = D // min(256, D)
     levels = seq_n.bit_length() - 1
-    gates = jnp.concatenate([input_gate, forget_gate], axis=1).astype(F32).T
     lanes = max(R, 128)
-    gates = jnp.pad(gates, ((0, -(2 * heads) % 8), (0, lanes - R)))
-    lines = gates.shape[0]
+    lines = 2 * heads
     segs = segment_ids.reshape(1, N)
     dma = pltpu.SemaphoreType.DMA
     vmem = pltpu.VMEM
@@ -591,9 +604,10 @@
     return pl.pallas_call(
         functools.partial(kernel, (seq_n, ten_n, heads, R, D)),
         out_shape=jax.ShapeDtypeStruct((R, inner), BF16),
-        in_specs=[whole, whole, whole, far, far, far, far],
-        out_specs=whole,
+        in_specs=[whole, whole, whole, whole, far, far, far, far],
+        out_specs=far,
         scratch_shapes=[
+            vmem((lines, lanes), F32),
             vmem((ten_n, lines, lanes), F32),
             vmem((N, D), BF16),
             vmem((N, C), BF16),
@@ -641,14 +655,16 @@
             dma((ten_n,)),
             dma,
             dma,
+            vmem((R, inner), BF16),
+            dma((heads,)),
         ],
         compiler_params=pltpu.CompilerParams(
-            collective_id=0, has_side_effects=True, vmem_limit_bytes=48 * 1024 * 1024
+            collective_id=0, has_side_effects=True, vmem_limit_bytes=LIMIT
         ),
         cost_estimate=pl.CostEstimate(
             flops=2 * N * (N * D + N * C + 2 * D * C), bytes_accessed=10 * R * inner, transcendentals=N * N
         ),
-    )(gates, segs, norm_gain.reshape(1, inner), queries, key_rows, values, output_gate)
+    )(input_gate.T, forget_gate.T, segs, norm_gain.reshape(1, inner), queries, key_rows, values, output_gate)
 
 
 def solution(mesh):

time: 113 us -> 110 us (0.973)
  local copies, waits for them, and re-layouts: 7.29 us -> 2.29 us
    unnamed x17 -> x1, local copies, waits for them, and re-layouts: 7.29 us -> 2.29 us
    pallas_call x1, Pallas kernels: 106 us -> 107 us  [on_device(): pl.pallas_call(functools.partial(kernel, (seq_n, ten_n, heads, R, D)), ou...]
where the time goes in v3:
time: 110 us; the launch traced here: 109 us
  Pallas kernels  107 us (97%)
  local copies, waits for them, and re-layouts  2.29 us (2%)
    pallas_call x1, Pallas kernels, on_device(): pl.pallas_call(functools.partial(kernel, (seq_n, ten_n, heads, R, D)), ou...  107 us
    unnamed x1, local copies, waits for them, and re-layouts  2.29 us

profile of v3, /device:TPU:17, one launch (start us, length us, event | category | flops | bytes accessed | tf_op | source)
XLA Modules:
  0.0 109.3 jit_solution(843807451030644436)
XLA Ops:
  0.0 107.0 %shard_map.82 = bf16[128,4096]{1,0:T(8,128)(2,1)} custom-call(bf16[4,128]{1,0:T(4,128)(2,1)} %bitcast.6, bf16[4,128]{1,0:T(4,128)(2,1)} %bitcast.7, s32[1,1024]{1,0:T(1,128)} %bitcast.5, f32[1,4096]{1,0:T(1,128)} %bitcast.4, bf16[128,4096]{1,0:T(8,128)(2,1)} %q_ref.1, bf16[128,4096]{1,0:T(8,128)(2,1)} %k_ref.1, bf16[128,4096]{1,0:T(8,128)(2,1)} %v_ref.1, ...), custom_call_target="tpu_custom_call" | custom-call | flops 5368709120 | bytes 5242880 | tf_op jit(solution)/shard_map/pallas_call | solution.py:604
  107.0 2.3 %copy.10 = bf16[128,4096]{1,0:T(8,128)(2,1)} copy(bf16[128,4096]{1,0:T(8,128)(2,1)} %shard_map.82) | data formatting | bytes 2097152

commit v4 on v3

--- a/solution.py
+++ b/solution.py
@@ -12,7 +12,7 @@
 F32 = jnp.float32
 BF16 = jnp.bfloat16
 EPS = 1e-05
-LIMIT = 63 * 1024 * 1024
+LIMIT = 62 * 1024 * 1024 + 512 * 1024
 NONE = -1e30
 
 
@@ -31,8 +31,8 @@
     dims,
     in_gate_ref,
     forget_ref,
-    seg_ref,
-    gain_ref,
+    seg_hbm,
+    gain_hbm,
     q_ref,
     k_ref,
     v_ref,
@@ -88,6 +88,9 @@
     k_own,
     out_v,
     w_sem,
+    seg_ref,
+    gain_ref,
+    small_sem,
 ):
     seq_n, ten_n, heads, R, D = dims
     group = ten_n // heads
@@ -116,8 +119,12 @@
     def val_cols(index):
         return pl.ds(pl.multiple_of(index * C, 128), C)
 
-    gates_ref[0:heads, 0:R] = in_gate_ref[...].astype(F32)
-    gates_ref[heads : 2 * heads, 0:R] = forget_ref[...].astype(F32)
+    small = [
+        pltpu.make_async_copy(a, b, small_sem.at[i])
+        for i, (a, b) in enumerate([(seg_hbm, seg_ref), (gain_hbm, gain_ref)])
+    ]
+    for copy in small:
+        copy.start()
     barrier = pltpu.get_barrier_semaphore()
     for d in range(1, ten_n):
         pl.semaphore_signal(
@@ -212,10 +219,12 @@
         )
 
     for d in range(1, ten_n):
+        val_copy(d).start()
+    gates_ref[0:heads, 0:R] = in_gate_ref[...].astype(F32)
+    gates_ref[heads : 2 * heads, 0:R] = forget_ref[...].astype(F32)
+    for d in range(1, ten_n):
         gate_copy(d).start()
     gates_all[t] = gates_ref[...]
-    for d in range(1, ten_n):
-        val_copy(d).start()
     own_val = pltpu.make_async_copy(v_ref.at[:, val_cols(t)], v_all.at[block(t)], v_recv.at[t])
     own_val.start()
     own_key = pltpu.make_async_copy(k_ref.at[:, head_cols(h)], k_all.at[block(t)], k_own)
@@ -269,6 +278,9 @@
         return jnp.broadcast_to(
             jnp.sum(jnp.where(eye, jnp.broadcast_to(row, (B, B)), 0.0), axis=1, keepdims=True), (B, 128)
         )
+
+    for copy in small:
+        copy.wait()
 
     def segs(b):
         return seg_ref[0:1, b * B : (b + 1) * B].astype(F32)
@@ -604,7 +616,7 @@
     return pl.pallas_call(
         functools.partial(kernel, (seq_n, ten_n, heads, R, D)),
         out_shape=jax.ShapeDtypeStruct((R, inner), BF16),
-        in_specs=[whole, whole, whole, whole, far, far, far, far],
+        in_specs=[whole, whole, far, far, far, far, far, far],
         out_specs=far,
         scratch_shapes=[
             vmem((lines, lanes), F32),
@@ -657,6 +669,9 @@
             dma,
             vmem((R, inner), BF16),
             dma((heads,)),
+            vmem((1, N), jnp.int32),
+            vmem((1, inner), F32),
+            dma((2,)),
         ],
         compiler_params=pltpu.CompilerParams(
             collective_id=0, has_side_effects=True, vmem_limit_bytes=LIMIT

time: 110 us -> 109 us (level)
  no operation moved by 1% of the time
where the time goes in v4:
time: 109 us
  Pallas kernels  107 us (98%)
  local copies, waits for them, and re-layouts  2.29 us (2%)
    pallas_call x1, Pallas kernels, on_device(): pl.pallas_call(functools.partial(kernel, (seq_n, ten_n, heads, R, D)), ou...  107 us
    unnamed x1, local copies, waits for them, and re-layouts  2.29 us

profile of v4, /device:TPU:17, one launch (start us, length us, event | category | flops | bytes accessed | tf_op | source)
XLA Modules:
  0.0 108.9 jit_solution(4837010641502044144)
XLA Ops:
  0.0 106.6 %shard_map.82 = bf16[128,4096]{1,0:T(8,128)(2,1)} custom-call(bf16[4,128]{1,0:T(4,128)(2,1)} %bitcast.6, bf16[4,128]{1,0:T(4,128)(2,1)} %bitcast.7, s32[1,1024]{1,0:T(1,128)} %bitcast.5, f32[1,4096]{1,0:T(1,128)} %bitcast.4, bf16[128,4096]{1,0:T(8,128)(2,1)} %q_ref.1, bf16[128,4096]{1,0:T(8,128)(2,1)} %k_ref.1, bf16[128,4096]{1,0:T(8,128)(2,1)} %v_ref.1, ...), custom_call_target="tpu_custom_call" | custom-call | flops 5368709120 | bytes 5242880 | tf_op jit(solution)/shard_map/pallas_call | solution.py:616
  106.6 2.3 %copy.10 = bf16[128,4096]{1,0:T(8,128)(2,1)} copy(bf16[128,4096]{1,0:T(8,128)(2,1)} %shard_map.82) | data formatting | bytes 2097152
